TPU v7x, 32 devices: a whole 2x2x4 slice. The times are simulated.
32 devices in a mesh: gx: 4 (over z), gy: 8 (over y, x, core).
Axes of the slice: x: 2, y: 2, z: 4, core: 2. Of those that a mesh axis runs over, the one named last changes fastest.
Arguments:
- seismic: float32 [512, 512, 256], P('gx', 'gy'), may hold values from -41 to 41, as said below
Outputs:
- shift_field: float32 [512, 512, 256], P('gx', 'gy')
- residual: float32 [512, 512, 256], P('gx', 'gy')
Inputs may be any that keep to these rules, and one draw needn't show every extreme that they name: `seismic`: recorded amplitudes of the window.
All inputs are finite; a program needn't handle non-finite values.
Results may differ from a plain program's by a relative error of at most 0.0003.
Values sent between devices are 32-bit elements; how exact they have to be, the bound alone decides.
A program may use at most 320 MiB of HBM per device.

v0:
```python
import jax
import jax.numpy as jnp
from jax import lax
from jax.sharding import PartitionSpec as P

NX = 512
NY = 512
ITERS = 2
damping = 0.001
floor_term = 0.5
highest = lax.Precision.HIGHEST


def extended(block, sides, width):
    for axis, dim in sides:
        count = lax.axis_size(axis)
        forward = [(i, i + 1) for i in range(count - 1)]
        backward = [(target, source) for source, target in forward]
        low = lax.ppermute(
            lax.slice_in_dim(block, block.shape[dim] - width, None, axis=dim), axis, forward
        )
        high = lax.ppermute(lax.slice_in_dim(block, 0, width, axis=dim), axis, backward)
        block = jnp.concatenate([low, block, high], axis=dim)
    return block


def cut(field, start, stop, axis):
    return lax.slice_in_dim(field, start, stop, axis=axis)


def smooth_axis(field, axis):
    length = field.shape[axis]
    return 0.25 * (
        cut(field, 0, length - 2, axis)
        + 2.0 * cut(field, 1, length - 1, axis)
        + cut(field, 2, length, axis)
    )


def pad_time(field):
    return jnp.pad(field, ((0, 0), (0, 0), (1, 1)))


def smooth_all(field):
    return smooth_axis(pad_time(smooth_axis(smooth_axis(field, 0), 1)), 2)


def tensor_fields(padded, inside_x, inside_y):
    mask = inside_x[:, None, None] * inside_y[None, :, None]
    grad_x = 0.5 * (padded[2:, 1:-1] - padded[:-2, 1:-1]) * mask
    grad_y = 0.5 * (padded[1:-1, 2:] - padded[1:-1, :-2]) * mask
    timed = pad_time(padded[1:-1, 1:-1])
    grad_t = 0.5 * (timed[:, :, 2:] - timed[:, :, :-2]) * mask
    cross_x = smooth_all(grad_x * grad_t)
    cross_y = smooth_all(grad_y * grad_t)
    along_t = smooth_all(grad_t * grad_t) + floor_term
    spread = smooth_all(grad_x * grad_x + grad_y * grad_y)
    return (-cross_x / along_t, -cross_y / along_t, along_t / (along_t + spread))


def cosine_table(order):
    freq = jnp.arange(order, dtype=jnp.float32)[:, None]
    place = jnp.arange(order, dtype=jnp.float32)[None, :]
    scale = jnp.where(freq == 0.0, jnp.sqrt(1.0 / order), jnp.sqrt(2.0 / order)).astype(jnp.float32)
    return scale * jnp.cos(jnp.pi * (place + 0.5) * freq / order)


def eigen_values(order):
    freq = jnp.arange(order, dtype=jnp.float32)
    return 2.0 - 2.0 * jnp.cos(jnp.pi * freq / order)


def combine_terms(field, upper_x, lower_x, upper_y, lower_y, weight_x, weight_y, prior_x, prior_y):
    return (
        damping * field
        + weight_x * (field - upper_x)
        + prior_x * (field - lower_x)
        + weight_y * (field - upper_y)
        + prior_y * (field - lower_y)
    )


def operate(field, weight_x, weight_y, prior_x, prior_y):
    padded = extended(field, (("gx", 0), ("gy", 1)), 1)
    return combine_terms(
        field,
        padded[2:, 1:-1],
        padded[:-2, 1:-1],
        padded[1:-1, 2:],
        padded[1:-1, :-2],
        weight_x,
        weight_y,
        prior_x,
        prior_y,
    )


def solve_front(front, table_x, table_y, plane_denom):
    hat = jnp.einsum("ki,tij->tkj", table_x, front, precision=highest)
    hat = jnp.einsum("lj,tkj->tkl", table_y, hat, precision=highest)
    hat = hat / plane_denom
    hat = jnp.einsum("lj,tkl->tkj", table_y, hat, precision=highest)
    return jnp.einsum("ki,tkj->tij", table_x, hat, precision=highest)


def slice_solve(whole, table_x, table_y, plane_denom):
    front = jnp.transpose(whole, (2, 0, 1))
    return jnp.transpose(solve_front(front, table_x, table_y, plane_denom), (1, 2, 0))


def reorder_back(back, rows_x, rows_y, parts_x, parts_y, depth):
    per = depth // (parts_x * parts_y)
    target = jnp.arange(depth, dtype=jnp.int32)
    outer = target // (parts_y * per)
    middle = target // per % parts_y
    source = middle * (parts_x * per) + outer * per + target % per
    select = (jnp.arange(depth, dtype=jnp.int32)[:, None] == source[None, :]).astype(jnp.float32)
    flat = back.reshape(rows_x * rows_y, depth)
    return jnp.dot(flat, select, precision=highest, preferred_element_type=jnp.float32).reshape(
        rows_x, rows_y, depth
    )


def inner(first, second):
    return lax.psum(jnp.sum(first * second), ("gx", "gy"))


def solve(rhs, apply_op, precondition):
    shift_field = jnp.zeros_like(rhs)
    residual = rhs
    precond = precondition(residual)
    direction = precond
    norm_now = inner(residual, precond)
    for step in range(ITERS):
        image = apply_op(direction)
        alpha = norm_now / lax.psum(jnp.sum(direction * image), ("gx", "gy"))
        shift_field = shift_field + alpha * direction
        residual = residual - alpha * image
        if step + 1 < ITERS:
            precond = precondition(residual)
            norm_next = inner(residual, precond)
            direction = precond + norm_next / norm_now * direction
            norm_now = norm_next
    return (shift_field, residual)


def per_device(seismic):
    rows_x, rows_y, depth = seismic.shape
    parts_x = lax.axis_size("gx")
    parts_y = lax.axis_size("gy")
    base_x = lax.axis_index("gx") * rows_x
    base_y = lax.axis_index("gy") * rows_y
    table_x = cosine_table(NX)
    table_y = cosine_table(NY)
    eigen_x = eigen_values(NX)
    eigen_y = eigen_values(NY)
    plane_denom = damping + eigen_x[:, None] + eigen_y[None, :]
    padded = extended(seismic, (("gx", 0), ("gy", 1)), 3)
    grid_x = base_x + jnp.arange(-2, rows_x + 2, dtype=jnp.int32)
    grid_y = base_y + jnp.arange(-2, rows_y + 2, dtype=jnp.int32)
    inside_x = ((grid_x >= 0) & (grid_x < NX)).astype(jnp.float32)
    inside_y = ((grid_y >= 0) & (grid_y < NY)).astype(jnp.float32)
    dip_x, dip_y, weight = tensor_fields(padded, inside_x, inside_y)
    edge_x = grid_x[1:-1]
    edge_y = grid_y[1:-1]
    keep_x = ((edge_x >= 0) & (edge_x < NX - 1)).astype(jnp.float32)
    keep_y = ((edge_y >= 0) & (edge_y < NY - 1)).astype(jnp.float32)
    weight_x = weight * keep_x[:, None, None]
    weight_y = weight * keep_y[None, :, None]
    flux_x = weight_x * dip_x
    flux_y = weight_y * dip_y
    rhs = flux_x[:-2, 1:-1] - flux_x[1:-1, 1:-1] + (flux_y[1:-1, :-2] - flux_y[1:-1, 1:-1])
    own_x = weight_x[1:-1, 1:-1]
    prior_x = weight_x[:-2, 1:-1]
    own_y = weight_y[1:-1, 1:-1]
    prior_y = weight_y[1:-1, :-2]

    def precondition(field):
        whole = lax.all_to_all(
            lax.all_to_all(field, "gx", split_axis=2, concat_axis=0, tiled=True),
            "gy",
            split_axis=2,
            concat_axis=1,
            tiled=True,
        )
        hat = slice_solve(whole, table_x, table_y, plane_denom)
        back = lax.all_to_all(
            lax.all_to_all(hat, "gx", split_axis=0, concat_axis=2, tiled=True),
            "gy",
            split_axis=1,
            concat_axis=2,
            tiled=True,
        )
        return reorder_back(back, rows_x, rows_y, parts_x, parts_y, depth)

    def apply_tiles(field):
        return operate(field, own_x, own_y, prior_x, prior_y)

    return solve(rhs, apply_tiles, precondition)


def solution(mesh):
    placed = (P("gx", "gy", None),)
    return jax.shard_map(
        per_device,
        mesh=mesh,
        in_specs=placed,
        out_specs=(P("gx", "gy", None), P("gx", "gy", None)),
        check_vma=False,
    )
```

profile of v0, /device:TPU:0, one launch (start us, length us, event | category | flops | bytes accessed | tf_op | source)
XLA Modules:
  0.0 2077.2 jit_solution(1720866723027973175)
XLA Ops:
  0.6 8.2 copy.195
  47.0 54.0 %fusion.77 = (f32[132,68,256]{2,0,1:T(8,128)}, f32[132,68,256]{2,0,1:T(8,128)}, f32[132,68,256]{2,0,1:T(8,128)}, f32[132,68,256]{2,0,1:T(8,128)}) fusion(f32[132,68]{0,1:T(8,128)S(1)} %multiply_multiply_fusion, f32[134,70,256]{2,0,1:T(8,128)} %copy-done.2, f32[132,68,256]{2,0,1:T(8,128)} %slice.298), kind=kLoop, calls=%fused_computation.146 | loop fusion | flops 36765696 | bytes 82758720 | tf_op jit(solution)/shard_map/mul | solution.py:55
  101.0 29.4 %fusion.6 = (f32[130,68,256]{2,0,1:T(8,128)}, f32[130,68,256]{2,0,1:T(8,128)}) fusion(f32[132,68,256]{2,0,1:T(8,128)} %get-tuple-element.29, f32[132,68,256]{2,0,1:T(8,128)} %get-tuple-element.30), kind=kLoop, calls=%fused_computation.23 | loop fusion | flops 18104320 | bytes 72417280 | tf_op jit(solution)/shard_map/mul | solution.py:33
  130.3 13.7 broadcast_multiply_fusion.4
  150.2 29.4 %fusion.2 = (f32[130,68,256]{2,0,1:T(8,128)}, f32[130,68,256]{2,0,1:T(8,128)}) fusion(f32[132,68,256]{2,0,1:T(8,128)} %get-tuple-element.27, f32[132,68,256]{2,0,1:T(8,128)} %get-tuple-element.28), kind=kLoop, calls=%fused_computation.15 | loop fusion | flops 18104320 | bytes 72417280 | tf_op jit(solution)/shard_map/mul | solution.py:33
  179.6 13.8 broadcast_multiply_fusion.3
  203.3 45.0 %fusion.24 = (f32[130,66,256]{2,0,1:T(8,128)}, f32[130,66,256]{2,0,1:T(8,128)}, f32[130,66,256]{2,0,1:T(8,128)}, f32[130,66,256]{2,0,1:T(8,128)}) fusion(f32[130,66,256]{2,0,1:T(8,128)} %broadcast_multiply_fusion.3, f32[130,68,256]{2,0,1:T(8,128)} %get-tuple-element.46, f32[130]{0:T(256)S(1)} %and_convert_fusion.1, f32[130,68,256]{2,0,1:T(8,128)S(1)} %bitcast.93, ...), kind=kLoop, calls=%fused_computation.47 | loop fusion | flops 61501440 | bytes 140575232 | tf_op jit(solution)/shard_map/mul | solution.py:170
  248.3 26.7 %fusion.30 = (f32[130,66,256]{2,0,1:T(8,128)}, f32[130,66,256]{2,0,1:T(8,128)}) fusion(f32[130,66,256]{2,0,1:T(8,128)} %get-tuple-element.24, f32[130,66,256]{2,0,1:T(8,128)} %broadcast_multiply_fusion.2, f32[130,68,256]{2,0,1:T(8,128)} %get-tuple-element.45, f32[130,66,256]{2,0,1:T(8,128)} %get-tuple-element.23, f32[66]{0:T(128)S(1)} %copy-done.9), kind=kLoop, calls=%fused_computation.53 | loop fusion | flops 24161280 | bytes 70287624 | tf_op jit(solution)/shard_map/mul | solution.py:171
  275.0 16.4 fusion.59
  291.3 8.7 copy.198
  300.0 185.5 %all_to_all.138 = f32[128,64,256]{0,1,2:T(8,128)S(1)} all-to-all(f32[128,64,256]{0,1,2:T(8,128)} %copy.198), channel_id=1, replica_groups=mesh['gx'=4,'gy'=8] {'gx'}, dimensions={2} | all-to-all | bytes 16777216 | tf_op jit(solution)/shard_map/all_to_all | solution.py:180
  490.0 11.4 all-to-all-start.1
  501.6 94.0 %all-to-all-done.1 = f32[512,64,64]{0,1,2:T(8,128)} async-done(((f32[512,64,64]{0,1,2:T(8,128)}), f32[512,64,64]{0,1,2:T(8,128)}, u32[]{:S(2)}, u32[]{:S(2)}) %all-to-all-start.1) | async-done | bytes 8388640 | tf_op jit(solution)/shard_map/all_to_all | solution.py:179
  595.6 8.1 copy.203
  603.7 22.6 %fusion.66 = f32[8,512,512]{2,1,0:T(8,128)S(1)} fusion(f32[512,512,8]{0,2,1:T(8,128)S(1)} %bitcast.102, f32[512]{0:T(512)S(1)} %get-tuple-element.49, f32[512]{0:T(512)S(1)} %get-tuple-element.50), kind=kOutput, calls=%fused_computation.117 | convolution fusion | flops 12885688320 | bytes 16781312 | tf_op jit(solution)/shard_map/ki,tij->tkj/dot_general | solution.py:99
  626.3 34.1 %fusion.64 = f32[8,512,512]{2,1,0:T(8,128)S(1)} fusion(f32[8,512,512]{2,1,0:T(8,128)S(1)} %fusion.66, f32[512]{0:T(512)S(1)} %get-tuple-element.49, f32[512]{0:T(512)S(1)} %get-tuple-element.50), kind=kOutput, calls=%fused_computation.115 | convolution fusion | flops 12885688320 | bytes 16781312 | tf_op jit(solution)/shard_map/lj,tkj->tkl/dot_general | solution.py:100
  660.4 19.8 fusion.72
  680.2 23.2 %convolution_bitcast_fusion.1 = f32[512,512,8]{0,1,2:T(8,128)} fusion(f32[8,512,512]{1,2,0:T(8,128)S(1)} %fusion.72, f32[512]{0:T(512)S(1)} %get-tuple-element.49, f32[512]{0:T(512)S(1)} %get-tuple-element.50), kind=kOutput, calls=%fused_computation.144 | convolution fusion | flops 12885688320 | bytes 16781312 | tf_op jit(solution)/shard_map/ki,tkj->tij/dot_general | solution.py:103
  703.4 10.5 copy.207
  713.9 184.9 %all_to_all.139 = f32[512,512,8]{1,2,0:T(8,128)S(1)} all-to-all(f32[512,512,8]{1,2,0:T(8,128)} %copy.207), channel_id=1, replica_groups=mesh['gx'=4,'gy'=8] {'gx'}, dimensions={0} | all-to-all | bytes 16777216 | tf_op jit(solution)/shard_map/all_to_all | solution.py:188
  903.2 11.0 copy.209
  919.2 94.1 %all-to-all-done.3 = f32[128,512,32]{0,2,1:T(8,128)} async-done(((f32[128,512,32]{0,2,1:T(8,128)}), f32[128,512,32]{0,2,1:T(8,128)}, u32[]{:S(2)}, u32[]{:S(2)}) %all-to-all-start.3) | async-done | bytes 8388640 | tf_op jit(solution)/shard_map/all_to_all | solution.py:187
  1013.3 12.3 copy.210
  1025.6 14.7 reshape.169
  1040.3 9.4 fusion.111
  1069.4 36.8 %multiply_reduce_fusion.2 = (f32[]{:T(128)}, f32[]{:T(128)}, f32[128,64,256]{2,0,1:T(8,128)}) fusion(f32[128,64,256]{2,1,0:T(8,128)} %bitcast.97, f32[128,64,256]{2,0,1:T(8,128)} %fusion.59, f32[128,64,256]{2,0,1:T(8,128)} %copy-done.7, f32[1,64,256]{2,0,1:T(1,128)S(1)} %copy.214, f32[1,64,256]{2,0,1:T(1,128)S(1)} %copy.216, ...), kind=kLoop, calls=%fused_computation.131 | loop fusion | flops 52428800 | bytes 67506184 | tf_op jit(solution)/shard_map/reduce_sum | solution.py:136
  1106.2 41.2 %all-reduce.5 = (f32[]{:T(128)}, f32[]{:T(128)}) all-reduce(f32[]{:T(128)} %get-tuple-element.15, f32[]{:T(128)} %get-tuple-element.14), channel_id=1, replica_groups=mesh['gx'=4,'gy'=8] {'gx','gy'}, use_global_device_ids=true, to_apply=%region_1.2 | all-reduce | flops 2 | bytes 16 | tf_op jit(solution)/shard_map/psum | solution.py:125
  1148.7 11.6 multiply_subtract_fusion.1
  1160.3 8.7 copy.226
  1169.1 186.9 %all_to_all.140 = f32[128,64,256]{0,1,2:T(8,128)S(1)} all-to-all(f32[128,64,256]{0,1,2:T(8,128)} %copy.226), channel_id=1, replica_groups=mesh['gx'=4,'gy'=8] {'gx'}, dimensions={2} | all-to-all | bytes 16777216 | tf_op jit(solution)/shard_map/all_to_all | solution.py:180
  1357.0 97.9 %all_to_all.141 = f32[512,64,64]{0,1,2:T(8,128)} all-to-all(f32[512,64,64]{0,1,2:T(8,128)S(1)} %bitcast.109), channel_id=1, replica_groups=mesh['gx'=4,'gy'=8] {'gy'}, dimensions={2} | all-to-all | bytes 16777216 | tf_op jit(solution)/shard_map/all_to_all | solution.py:179
  1463.1 22.6 %fusion.62 = f32[8,512,512]{2,1,0:T(8,128)S(1)} fusion(f32[512,512,8]{0,2,1:T(8,128)S(1)} %bitcast.103, f32[512]{0:T(512)S(1)} %get-tuple-element.49, f32[512]{0:T(512)S(1)} %get-tuple-element.50), kind=kOutput, calls=%fused_computation.113 | convolution fusion | flops 12885688320 | bytes 16781312 | tf_op jit(solution)/shard_map/ki,tij->tkj/dot_general | solution.py:99
  1485.7 34.1 %fusion.60 = f32[8,512,512]{2,1,0:T(8,128)S(1)} fusion(f32[8,512,512]{2,1,0:T(8,128)S(1)} %fusion.62, f32[512]{0:T(512)S(1)} %get-tuple-element.49, f32[512]{0:T(512)S(1)} %get-tuple-element.50), kind=kOutput, calls=%fused_computation.111 | convolution fusion | flops 12885688320 | bytes 16781312 | tf_op jit(solution)/shard_map/lj,tkj->tkl/dot_general | solution.py:100
  1519.8 19.8 fusion.70
  1539.6 23.2 %convolution_bitcast_fusion = f32[512,512,8]{0,1,2:T(8,128)} fusion(f32[8,512,512]{1,2,0:T(8,128)S(1)} %fusion.70, f32[512]{0:T(512)S(1)} %get-tuple-element.49, f32[512]{0:T(512)S(1)} %get-tuple-element.50), kind=kOutput, calls=%fused_computation.143 | convolution fusion | flops 12885688320 | bytes 16781312 | tf_op jit(solution)/shard_map/ki,tkj->tij/dot_general | solution.py:103
  1562.8 10.4 copy.235
  1573.3 187.0 %all_to_all.142 = f32[512,512,8]{1,2,0:T(8,128)S(1)} all-to-all(f32[512,512,8]{1,2,0:T(8,128)} %copy.235), channel_id=1, replica_groups=mesh['gx'=4,'gy'=8] {'gx'}, dimensions={0} | all-to-all | bytes 16777216 | tf_op jit(solution)/shard_map/all_to_all | solution.py:188
  1764.5 11.0 copy.237
  1775.5 97.8 %all_to_all.143 = f32[128,512,32]{0,2,1:T(8,128)S(1)} all-to-all(f32[128,512,32]{0,2,1:T(8,128)} %copy.237), channel_id=1, replica_groups=mesh['gx'=4,'gy'=8] {'gy'}, dimensions={1} | all-to-all | bytes 16777216 | tf_op jit(solution)/shard_map/all_to_all | solution.py:187
  1879.8 14.6 multiply_reduce_fusion.1
  1894.3 38.5 %psum.30 = f32[]{:T(128)} all-reduce(f32[]{:T(128)} %get-tuple-element.43), channel_id=1, replica_groups=mesh['gx'=4,'gy'=8] {'gx','gy'}, use_global_device_ids=true, to_apply=%region_5.6 | all-reduce | flops 1 | bytes 8 | tf_op jit(solution)/shard_map/psum | solution.py:125
  1934.2 14.2 multiply_add_fusion.2
  1964.1 20.2 multiply_reduce_fusion
  1984.3 45.3 %psum.31 = f32[]{:T(128)} all-reduce(f32[]{:T(128)} %get-tuple-element.18), channel_id=1, replica_groups=mesh['gx'=4,'gy'=8] {'gx','gy'}, use_global_device_ids=true, to_apply=%region_7.8 | all-reduce | flops 1 | bytes 8 | tf_op jit(solution)/shard_map/psum | solution.py:136
  2030.9 14.2 multiply_add_fusion.1
  2045.1 11.6 multiply_subtract_fusion
  2056.7 12.0 copy.242
  2068.7 8.3 copy.241
  (94 shorter events, 123.5 us)
Async XLA Ops:
  8.9 3.4 copy-start.5
  12.4 10.5 collective-permute-start
  17.3 9.7 collective-permute-start.1
  18.7 16.2 copy-start.6
  28.2 3.8 collective-permute-start.2
  29.5 5.4 collective-permute-start.3
  38.7 3.7 copy-start.2
  130.3 14.9 copy-start
  179.6 14.9 copy-start.1
  179.6 20.3 slice-start
  179.6 20.3 slice-start.1
  179.6 21.7 %slice-start.3 = ((s8[9469952]{0:T(1024)(128)(4,1)}), s8[4194304]{0:T(1024)(128)(4,1)S(1)}, s32[]{:S(2)}) async-start(s8[9469952]{0:T(1024)(128)(4,1)} %bitcast.94), calls=%async_computation.11 | async-start | bytes 8388608
  179.6 22.9 %slice-start.4 = ((s8[9469952]{0:T(1024)(128)(4,1)}), s8[4194304]{0:T(1024)(128)(4,1)S(1)}, s32[]{:S(2)}) async-start(s8[9469952]{0:T(1024)(128)(4,1)} %bitcast.94), calls=%async_computation.12 | async-start | bytes 8388608
  194.5 8.5 slice-start.2
  194.5 8.8 slice-start.5
  203.3 45.0 %copy-start.9 = (f32[66]{0:T(128)S(1)}, f32[66]{0:T(128)}, u32[]{:S(2)}) copy-start(f32[66]{0:T(128)} %and_convert_fusion) | copy-start | bytes 796
  490.0 105.6 %all-to-all-start.1 = ((f32[512,64,64]{0,1,2:T(8,128)}), f32[512,64,64]{0,1,2:T(8,128)}, u32[]{:S(2)}, u32[]{:S(2)}) async-start(f32[512,64,64]{0,1,2:T(8,128)} %bitcast.104), calls=%async_computation.1 | async-start | bytes 16777216 | tf_op jit(solution)/shard_map/all_to_all | solution.py:179
  914.3 99.0 %all-to-all-start.3 = ((f32[128,512,32]{0,2,1:T(8,128)}), f32[128,512,32]{0,2,1:T(8,128)}, u32[]{:S(2)}, u32[]{:S(2)}) async-start(f32[128,512,32]{0,2,1:T(8,128)} %copy.209), calls=%async_computation.3 | async-start | bytes 16777216 | tf_op jit(solution)/shard_map/all_to_all | solution.py:187
  1049.7 11.4 copy-start.3
  1049.7 11.1 collective-permute-start.4
  1051.0 9.9 collective-permute-start.5
  1060.9 3.3 copy-start.7
  1064.1 4.3 collective-permute-start.6
  1065.4 4.0 collective-permute-start.7
  1873.3 5.3 slice-start.6
  1873.3 6.5 slice-start.7
  1948.3 15.8 copy-start.4
  1949.8 6.4 collective-permute-start.8
  1951.3 6.4 collective-permute-start.9
  1958.8 4.3 collective-permute-start.10
  1960.1 4.0 collective-permute-start.11
  2056.7 12.0 copy-start.8
where the time goes:
time: 2080 us
  blocking collectives  1060 us (51%)
  other arithmetic  354 us (17%)
  matrix products  223 us (11%)
  waiting for transfers between devices  203 us (10%)
  local copies, waits for them, and re-layouts  180 us (9%)
  starting transfers between devices  46.8 us (2%)
    all_to_all x2, blocking collectives, precondition(): lax.all_to_all(field, 'gx', split_axis=2, concat_axis=0, tiled=True)  372 us
    all_to_all x2, blocking collectives, precondition(): lax.all_to_all(hat, 'gx', split_axis=0, concat_axis=2, tiled=True)  372 us
    all_to_all x1, blocking collectives, precondition(): lax.all_to_all(lax.all_to_all(field, 'gx', split_axis=2, concat_axis=0, t...  97.9 us
    all_to_all x1, blocking collectives, precondition(): lax.all_to_all(lax.all_to_all(hat, 'gx', split_axis=0, concat_axis=2, til...  97.8 us
    mul x6, other arithmetic, smooth_axis(): 0.25 * (cut(field, 0, length - 2, axis) + 2.0 * cut(field, 1, length - 1,...  96.6 us
    all_to_all x1, waiting for transfers between devices, precondition(): lax.all_to_all(lax.all_to_all(hat, 'gx', split_axis=0, concat_axis=2, til...  94.1 us
    all_to_all x1, waiting for transfers between devices, precondition(): lax.all_to_all(lax.all_to_all(field, 'gx', split_axis=2, concat_axis=0, t...  94 us
    psum x2, blocking collectives, inner(): return lax.psum(jnp.sum(first * second), ('gx', 'gy'))  79.7 us
  transfers between devices with their start and end apart: 14, of which 9 were waited for; matrix products, arithmetic and copies ran while one was open for 0% of the time, Pallas kernels for 0%

commit v1 on v0

--- a/solution.py
+++ b/solution.py
@@ -176,13 +176,20 @@
     prior_y = weight_y[1:-1, :-2]
 
     def precondition(field):
-        whole = lax.all_to_all(
-            lax.all_to_all(field, "gx", split_axis=2, concat_axis=0, tiled=True),
-            "gy",
-            split_axis=2,
-            concat_axis=1,
-            tiled=True,
-        )
+        array = lax.all_to_all(field, "gx", split_axis=2, concat_axis=0, tiled=True)
+        ways, here = (lax.axis_size("gy"), lax.axis_index("gy"))
+        width_2 = array.shape[2] // ways
+        dims = list(array.shape)
+        dims[2] = width_2
+        height = dims[1]
+        dims[1] = height * ways
+        full = jnp.zeros(dims, array.dtype)
+        for mask_2 in range(ways):
+            part = lax.dynamic_slice_in_dim(array, (here ^ mask_2) * width_2, width_2, axis=2)
+            if mask_2:
+                part = lax.ppermute(part, "gy", [(d, d ^ mask_2) for d in range(ways)])
+            full = lax.dynamic_update_slice_in_dim(full, part, (here ^ mask_2) * height, axis=1)
+        whole = full
         hat = slice_solve(whole, table_x, table_y, plane_denom)
         back = lax.all_to_all(
             lax.all_to_all(hat, "gx", split_axis=0, concat_axis=2, tiled=True),

time: 2080 us -> 2120 us (1.019)
  blocking collectives: 1060 us -> 791 us
  waiting for transfers between devices: 203 us -> 457 us
  local copies, waits for them, and re-layouts: 180 us -> 228 us
    all_to_all x3 -> x1, blocking collectives: 470 us -> 190 us  [precondition(): array = lax.all_to_all(field, 'gx', split_axis=2, concat_axis=0, tiled=True)]
    ppermute x0 -> x14, waiting for transfers between devices: none -> 165 us  [precondition(): part = lax.ppermute(part, 'gy', [(d, d ^ mask_2) for d in range(ways)])]
    all_to_all x1, waiting for transfers between devices: 94 us -> 183 us  [precondition(): array = lax.all_to_all(field, 'gx', split_axis=2, concat_axis=0, tiled=True)]
    all_to_all x4, local copies, waits for them, and re-layouts: 21.8 us -> 45.5 us  [precondition(): array = lax.all_to_all(field, 'gx', split_axis=2, concat_axis=0, tiled=True)]
    unnamed x39 -> x43, local copies, waits for them, and re-layouts: 45.5 us -> 44.5 us
  transfers between devices with their start and end apart: 14 -> 28, of which waited for: 9 -> 15; matrix products, arithmetic and copies ran while one was open for 0% -> 1% of each run, Pallas kernels for 0% -> 0%
where the time goes in v1:
time: 2120 us; the launch traced here: 2110 us
  blocking collectives  791 us (37%)
  waiting for transfers between devices  457 us (22%)
  other arithmetic  355 us (17%)
  local copies, waits for them, and re-layouts  228 us (11%)
  matrix products  216 us (10%)
  starting transfers between devices  59.8 us (3%)
    all_to_all x2, blocking collectives, precondition(): lax.all_to_all(hat, 'gx', split_axis=0, concat_axis=2, tiled=True)  377 us
    all_to_all x1, blocking collectives, precondition(): array = lax.all_to_all(field, 'gx', split_axis=2, concat_axis=0, tiled=True)  190 us
    all_to_all x1, waiting for transfers between devices, precondition(): array = lax.all_to_all(field, 'gx', split_axis=2, concat_axis=0, tiled=True)  183 us
    ppermute x14, waiting for transfers between devices, precondition(): part = lax.ppermute(part, 'gy', [(d, d ^ mask_2) for d in range(ways)])  165 us
    all_to_all x1, blocking collectives, precondition(): lax.all_to_all(lax.all_to_all(hat, 'gx', split_axis=0, concat_axis=2, til...  98.1 us
    mul x6, other arithmetic, smooth_axis(): 0.25 * (cut(field, 0, length - 2, axis) + 2.0 * cut(field, 1, length - 1,...  96.8 us
    all_to_all x1, waiting for transfers between devices, precondition(): lax.all_to_all(lax.all_to_all(hat, 'gx', split_axis=0, concat_axis=2, til...  94.1 us
    psum x2, blocking collectives, inner(): return lax.psum(jnp.sum(first * second), ('gx', 'gy'))  80.1 us
  transfers between devices with their start and end apart: 28, of which 15 were waited for; matrix products, arithmetic and copies ran while one was open for 1% of the time, Pallas kernels for 0%

profile of v1, /device:TPU:0, one launch (start us, length us, event | category | flops | bytes accessed | tf_op | source)
XLA Modules:
  0.0 2111.4 jit_solution(2778839904464890453)
XLA Ops:
  47.0 53.7 %fusion.75 = (f32[132,68,256]{2,0,1:T(8,128)}, f32[132,68,256]{2,0,1:T(8,128)}, f32[132,68,256]{2,0,1:T(8,128)}, f32[132,68,256]{2,0,1:T(8,128)}) fusion(f32[132,68]{0,1:T(8,128)S(1)} %multiply_multiply_fusion, f32[134,70,256]{2,0,1:T(8,128)} %copy-done.2, f32[132,68,256]{2,0,1:T(8,128)} %slice.298), kind=kLoop, calls=%fused_computation.142 | loop fusion | flops 36765696 | bytes 82758720 | tf_op jit(solution)/shard_map/mul | solution.py:55
  100.7 29.4 %fusion.6 = (f32[130,68,256]{2,0,1:T(8,128)}, f32[130,68,256]{2,0,1:T(8,128)}) fusion(f32[132,68,256]{2,0,1:T(8,128)} %get-tuple-element.29, f32[132,68,256]{2,0,1:T(8,128)} %get-tuple-element.30), kind=kLoop, calls=%fused_computation.23 | loop fusion | flops 18104320 | bytes 72417280 | tf_op jit(solution)/shard_map/mul | solution.py:33
  130.1 13.7 broadcast_multiply_fusion.4
  150.0 29.6 %fusion.2 = (f32[130,68,256]{2,0,1:T(8,128)}, f32[130,68,256]{2,0,1:T(8,128)}) fusion(f32[132,68,256]{2,0,1:T(8,128)} %get-tuple-element.27, f32[132,68,256]{2,0,1:T(8,128)} %get-tuple-element.28), kind=kLoop, calls=%fused_computation.15 | loop fusion | flops 18104320 | bytes 72417280 | tf_op jit(solution)/shard_map/mul | solution.py:33
  179.6 13.8 broadcast_multiply_fusion.3
  203.3 45.1 %fusion.24 = (f32[130,66,256]{2,0,1:T(8,128)}, f32[130,66,256]{2,0,1:T(8,128)}, f32[130,66,256]{2,0,1:T(8,128)}, f32[130,66,256]{2,0,1:T(8,128)}) fusion(f32[130,66,256]{2,0,1:T(8,128)} %broadcast_multiply_fusion.3, f32[130,68,256]{2,0,1:T(8,128)} %get-tuple-element.62, f32[130]{0:T(256)S(1)} %and_convert_fusion.1, f32[130,68,256]{2,0,1:T(8,128)S(1)} %bitcast.81, ...), kind=kLoop, calls=%fused_computation.47 | loop fusion | flops 61501440 | bytes 140575232 | tf_op jit(solution)/shard_map/mul | solution.py:170
  248.4 27.0 %fusion.30 = (f32[130,66,256]{2,0,1:T(8,128)}, f32[130,66,256]{2,0,1:T(8,128)}) fusion(f32[130,66,256]{2,0,1:T(8,128)} %get-tuple-element.24, f32[130,66,256]{2,0,1:T(8,128)} %broadcast_multiply_fusion.2, f32[130,68,256]{2,0,1:T(8,128)} %get-tuple-element.61, f32[130,66,256]{2,0,1:T(8,128)} %get-tuple-element.23, f32[66]{0:T(128)S(1)} %copy-done.11), kind=kLoop, calls=%fused_computation.53 | loop fusion | flops 24161280 | bytes 70287624 | tf_op jit(solution)/shard_map/mul | solution.py:171
  275.4 16.4 fusion.59
  306.2 183.4 %all-to-all-done = f32[128,64,256]{0,1,2:T(8,128)} async-done(((f32[128,64,256]{0,1,2:T(8,128)}), f32[128,64,256]{0,1,2:T(8,128)}, u32[]{:S(2)}, u32[]{:S(2)}) %all-to-all-start) | async-done | bytes 8388640 | tf_op jit(solution)/shard_map/all_to_all | solution.py:179
  489.6 12.2 copy.226
  501.7 10.7 all_to_all.77
  534.7 16.9 collective-permute-done.5
  553.7 20.0 collective-permute-done.6
  575.1 44.5 %collective-permute-done.8 = f32[512,64,8]{0,2,1:T(8,128)S(1)} collective-permute-done((f32[512,64,8]{0,2,1:T(8,128)}, f32[512,64,8]{0,2,1:T(8,128)S(1)}, u32[]{:S(2)}, u32[]{:S(2)}) %collective-permute-start.8) | collective-permute-done | bytes 1048608 | tf_op jit(solution)/shard_map/ppermute | solution.py:190
  621.8 18.5 fusion.66
  640.3 34.1 %fusion.64 = f32[8,512,512]{2,1,0:T(8,128)S(1)} fusion(f32[8,512,512]{2,1,0:T(8,128)S(1)} %fusion.66, f32[512]{0:T(512)S(1)} %get-tuple-element.65, f32[512]{0:T(512)S(1)} %get-tuple-element.66), kind=kOutput, calls=%fused_computation.113 | convolution fusion | flops 12885688320 | bytes 16781312 | tf_op jit(solution)/shard_map/lj,tkj->tkl/dot_general | solution.py:100
  674.4 19.8 fusion.70
  694.2 23.4 %convolution_bitcast_fusion.1 = f32[512,512,8]{0,1,2:T(8,128)} fusion(f32[8,512,512]{1,2,0:T(8,128)S(1)} %fusion.70, f32[512]{0:T(512)S(1)} %get-tuple-element.65, f32[512]{0:T(512)S(1)} %get-tuple-element.66), kind=kOutput, calls=%fused_computation.140 | convolution fusion | flops 12885688320 | bytes 16781312 | tf_op jit(solution)/shard_map/ki,tkj->tij/dot_general | solution.py:103
  717.6 10.5 copy.237
  728.1 188.4 %all_to_all.102 = f32[512,512,8]{1,2,0:T(8,128)S(1)} all-to-all(f32[512,512,8]{1,2,0:T(8,128)} %copy.237), channel_id=1, replica_groups=mesh['gx'=4,'gy'=8] {'gx'}, dimensions={0} | all-to-all | bytes 16777216 | tf_op jit(solution)/shard_map/all_to_all | solution.py:195
  921.0 11.0 copy.239
  937.0 94.1 %all-to-all-done.2 = f32[128,512,32]{0,2,1:T(8,128)} async-done(((f32[128,512,32]{0,2,1:T(8,128)}), f32[128,512,32]{0,2,1:T(8,128)}, u32[]{:S(2)}, u32[]{:S(2)}) %all-to-all-start.2) | async-done | bytes 8388640 | tf_op jit(solution)/shard_map/all_to_all | solution.py:194
  1031.0 12.3 copy.240
  1043.3 14.7 reshape.169
  1087.1 36.8 %multiply_reduce_fusion.2 = (f32[]{:T(128)}, f32[]{:T(128)}, f32[128,64,256]{2,0,1:T(8,128)}) fusion(f32[128,64,256]{2,1,0:T(8,128)} %bitcast.85, f32[128,64,256]{2,0,1:T(8,128)} %fusion.59, f32[128,64,256]{2,0,1:T(8,128)} %copy-done.7, f32[1,64,256]{2,0,1:T(1,128)S(1)} %copy.244, f32[1,64,256]{2,0,1:T(1,128)S(1)} %copy.246, ...), kind=kLoop, calls=%fused_computation.127 | loop fusion | flops 52428800 | bytes 67506184 | tf_op jit(solution)/shard_map/reduce_sum | solution.py:136
  1123.9 41.7 %all-reduce.5 = (f32[]{:T(128)}, f32[]{:T(128)}) all-reduce(f32[]{:T(128)} %get-tuple-element.15, f32[]{:T(128)} %get-tuple-element.14), channel_id=1, replica_groups=mesh['gx'=4,'gy'=8] {'gx','gy'}, use_global_device_ids=true, to_apply=%region_1.2 | all-reduce | flops 2 | bytes 16 | tf_op jit(solution)/shard_map/psum | solution.py:125
  1166.8 11.6 multiply_subtract_fusion.1
  1187.1 190.2 %all_to_all.103 = f32[128,64,256]{0,1,2:T(8,128)} all-to-all(f32[128,64,256]{0,1,2:T(8,128)} %copy.256), channel_id=1, replica_groups=mesh['gx'=4,'gy'=8] {'gx'}, dimensions={2} | all-to-all | bytes 16777216 | tf_op jit(solution)/shard_map/all_to_all | solution.py:179
  1377.3 12.1 copy.258
  1389.4 10.5 all_to_all.88
  1413.0 18.2 collective-permute-done.16
  1432.5 20.7 collective-permute-done.17
  1454.5 44.8 %collective-permute-done.19 = f32[512,64,8]{0,2,1:T(8,128)S(1)} collective-permute-done((f32[512,64,8]{0,2,1:T(8,128)S(1)}, f32[512,64,8]{0,2,1:T(8,128)S(1)}, u32[]{:S(2)}, u32[]{:S(2)}) %collective-permute-start.19) | collective-permute-done | bytes 1048608 | tf_op jit(solution)/shard_map/ppermute | solution.py:190
  1501.4 18.7 fusion.62
  1520.2 34.1 %fusion.60 = f32[8,512,512]{2,1,0:T(8,128)S(1)} fusion(f32[8,512,512]{2,1,0:T(8,128)S(1)} %fusion.62, f32[512]{0:T(512)S(1)} %get-tuple-element.65, f32[512]{0:T(512)S(1)} %get-tuple-element.66), kind=kOutput, calls=%fused_computation.109 | convolution fusion | flops 12885688320 | bytes 16781312 | tf_op jit(solution)/shard_map/lj,tkj->tkl/dot_general | solution.py:100
  1554.3 19.8 fusion.68
  1574.1 23.2 %convolution_bitcast_fusion = f32[512,512,8]{0,1,2:T(8,128)} fusion(f32[8,512,512]{1,2,0:T(8,128)S(1)} %fusion.68, f32[512]{0:T(512)S(1)} %get-tuple-element.65, f32[512]{0:T(512)S(1)} %get-tuple-element.66), kind=kOutput, calls=%fused_computation.139 | convolution fusion | flops 12885688320 | bytes 16781312 | tf_op jit(solution)/shard_map/ki,tkj->tij/dot_general | solution.py:103
  1607.7 188.4 %all_to_all.104 = f32[512,512,8]{1,2,0:T(8,128)S(1)} all-to-all(f32[512,512,8]{1,2,0:T(8,128)} %copy.269), channel_id=1, replica_groups=mesh['gx'=4,'gy'=8] {'gx'}, dimensions={0} | all-to-all | bytes 16777216 | tf_op jit(solution)/shard_map/all_to_all | solution.py:195
  1800.4 11.0 copy.271
  1811.4 98.1 %all_to_all.105 = f32[128,512,32]{0,2,1:T(8,128)S(1)} all-to-all(f32[128,512,32]{0,2,1:T(8,128)} %copy.271), channel_id=1, replica_groups=mesh['gx'=4,'gy'=8] {'gy'}, dimensions={1} | all-to-all | bytes 16777216 | tf_op jit(solution)/shard_map/all_to_all | solution.py:194
  1913.8 14.6 multiply_reduce_fusion.1
  1928.4 38.5 %psum.30 = f32[]{:T(128)} all-reduce(f32[]{:T(128)} %get-tuple-element.59), channel_id=1, replica_groups=mesh['gx'=4,'gy'=8] {'gx','gy'}, use_global_device_ids=true, to_apply=%region_5.6 | all-reduce | flops 1 | bytes 8 | tf_op jit(solution)/shard_map/psum | solution.py:125
  1968.3 14.2 multiply_add_fusion.2
  1998.2 20.2 multiply_reduce_fusion
  2018.4 45.3 %psum.31 = f32[]{:T(128)} all-reduce(f32[]{:T(128)} %get-tuple-element.18), channel_id=1, replica_groups=mesh['gx'=4,'gy'=8] {'gx','gy'}, use_global_device_ids=true, to_apply=%region_7.8 | all-reduce | flops 1 | bytes 8 | tf_op jit(solution)/shard_map/psum | solution.py:136
  2065.1 14.2 multiply_add_fusion.1
  2079.4 11.6 multiply_subtract_fusion
  2091.0 12.0 copy.276
  (144 shorter events, 212.5 us)
Async XLA Ops:
  8.9 3.4 copy-start.5
  12.4 10.5 collective-permute-start
  17.3 9.7 collective-permute-start.1
  18.7 16.2 copy-start.6
  28.2 3.8 collective-permute-start.2
  29.5 5.4 collective-permute-start.3
  38.7 3.8 copy-start.2
  130.1 14.9 copy-start
  179.6 14.9 copy-start.1
  179.6 20.3 slice-start
  179.6 20.3 slice-start.1
  179.6 21.7 %slice-start.3 = ((s8[9469952]{0:T(1024)(128)(4,1)}), s8[4194304]{0:T(1024)(128)(4,1)S(1)}, s32[]{:S(2)}) async-start(s8[9469952]{0:T(1024)(128)(4,1)} %bitcast.82), calls=%async_computation.9 | async-start | bytes 8388608
  179.6 22.9 %slice-start.4 = ((s8[9469952]{0:T(1024)(128)(4,1)}), s8[4194304]{0:T(1024)(128)(4,1)S(1)}, s32[]{:S(2)}) async-start(s8[9469952]{0:T(1024)(128)(4,1)} %bitcast.82), calls=%async_computation.10 | async-start | bytes 8388608
  194.5 8.5 slice-start.2
  194.5 8.8 slice-start.5
  203.3 45.1 %copy-start.11 = (f32[66]{0:T(128)S(1)}, f32[66]{0:T(128)}, u32[]{:S(2)}) copy-start(f32[66]{0:T(128)} %and_convert_fusion) | copy-start | bytes 796
  300.5 189.1 %all-to-all-start = ((f32[128,64,256]{0,1,2:T(8,128)}), f32[128,64,256]{0,1,2:T(8,128)}, u32[]{:S(2)}, u32[]{:S(2)}) async-start(f32[128,64,256]{0,1,2:T(8,128)} %copy.224), calls=%async_computation | async-start | bytes 16777216 | tf_op jit(solution)/shard_map/all_to_all | solution.py:179
  518.8 12.1 collective-permute-start.4
  519.7 31.9 %collective-permute-start.5 = (f32[512,64,8]{0,2,1:T(8,128)}, f32[512,64,8]{0,2,1:T(8,128)}, u32[]{:S(2)}, u32[]{:S(2)}) collective-permute-start(f32[512,64,8]{0,2,1:T(8,128)} %get-tuple-element.54), channel_id=1, source_target_pairs={{0,2},{1,3},{2,0},{3,1},{4,6},{5,7},{6,4},{7,5},{8,10},{9,11},{10,... | collective-permute-start | bytes 3145736 | tf_op jit(solution)/shard_map/ppermute | solution.py:190
  527.4 46.3 %collective-permute-start.6 = (f32[512,64,8]{0,2,1:T(8,128)}, f32[512,64,8]{0,2,1:T(8,128)S(1)}, u32[]{:S(2)}, u32[]{:S(2)}) collective-permute-start(f32[512,64,8]{0,2,1:T(8,128)} %get-tuple-element.53), channel_id=1, source_target_pairs={{0,3},{1,2},{2,1},{3,0},{4,7},{5,6},{6,5},{7,4},{8,11},{9,10},{10,... | collective-permute-start | bytes 3145736 | tf_op jit(solution)/shard_map/ppermute | solution.py:190
  527.6 146.8 %copy-start.9 = (f32[512,512]{1,0:T(8,128)}, f32[512,512]{1,0:T(8,128)S(1)}, u32[]{:S(2)}) copy-start(f32[512,512]{1,0:T(8,128)S(1)} %broadcast_add_fusion) | copy-start | bytes 3145732
  527.6 46.7 %collective-permute-start.7 = (f32[512,64,8]{0,2,1:T(8,128)}, f32[512,64,8]{0,2,1:T(8,128)S(1)}, u32[]{:S(2)}, u32[]{:S(2)}) collective-permute-start(f32[512,64,8]{0,2,1:T(8,128)} %get-tuple-element.52), channel_id=1, source_target_pairs={{0,4},{1,5},{2,6},{3,7},{4,0},{5,1},{6,2},{7,3},{8,12},{9,13},{10,... | collective-permute-start | bytes 3145736 | tf_op jit(solution)/shard_map/ppermute | solution.py:190
  528.8 90.8 %collective-permute-start.8 = (f32[512,64,8]{0,2,1:T(8,128)}, f32[512,64,8]{0,2,1:T(8,128)S(1)}, u32[]{:S(2)}, u32[]{:S(2)}) collective-permute-start(f32[512,64,8]{0,2,1:T(8,128)} %get-tuple-element.51), channel_id=1, source_target_pairs={{0,5},{1,4},{2,7},{3,6},{4,1},{5,0},{6,3},{7,2},{8,13},{9,12},{10,... | collective-permute-start | bytes 3145736 | tf_op jit(solution)/shard_map/ppermute | solution.py:190
  530.9 89.4 %collective-permute-start.9 = (f32[512,64,8]{0,2,1:T(8,128)S(1)}, f32[512,64,8]{0,2,1:T(8,128)S(1)}, u32[]{:S(2)}, u32[]{:S(2)}) collective-permute-start(f32[512,64,8]{0,2,1:T(8,128)S(1)} %get-tuple-element.50), channel_id=1, source_target_pairs={{0,6},{1,7},{2,4},{3,5},{4,2},{5,3},{6,0},{7,1},{8,14},{9,15},{10,... | collective-permute-start | bytes 3145736 | tf_op jit(solution)/shard_map/ppermute | solution.py:190
  551.6 69.4 %collective-permute-start.10 = (f32[512,64,8]{0,2,1:T(8,128)S(1)}, f32[512,64,8]{0,2,1:T(8,128)S(1)}, u32[]{:S(2)}, u32[]{:S(2)}) collective-permute-start(f32[512,64,8]{0,2,1:T(8,128)S(1)} %get-tuple-element.49), channel_id=1, source_target_pairs={{0,7},{1,6},{2,5},{3,4},{4,3},{5,2},{6,1},{7,0},{8,15},{9,14},{10,... | collective-permute-start | bytes 3145736 | tf_op jit(solution)/shard_map/ppermute | solution.py:190
  932.0 99.0 %all-to-all-start.2 = ((f32[128,512,32]{0,2,1:T(8,128)}), f32[128,512,32]{0,2,1:T(8,128)}, u32[]{:S(2)}, u32[]{:S(2)}) async-start(f32[128,512,32]{0,2,1:T(8,128)} %copy.239), calls=%async_computation.2 | async-start | bytes 16777216 | tf_op jit(solution)/shard_map/all_to_all | solution.py:194
  1067.5 11.0 copy-start.3
  1067.5 11.0 collective-permute-start.11
  1068.8 9.7 collective-permute-start.12
  1078.4 3.3 copy-start.7
  1081.7 4.3 collective-permute-start.13
  1083.0 4.0 collective-permute-start.14
  1404.3 6.5 collective-permute-start.15
  1404.4 26.8 %collective-permute-start.16 = (f32[512,64,8]{0,2,1:T(8,128)S(1)}, f32[512,64,8]{0,2,1:T(8,128)S(1)}, u32[]{:S(2)}, u32[]{:S(2)}) collective-permute-start(f32[512,64,8]{0,2,1:T(8,128)S(1)} %get-tuple-element.44), channel_id=1, source_target_pairs={{0,2},{1,3},{2,0},{3,1},{4,6},{5,7},{6,4},{7,5},{8,10},{9,11},{10,... | collective-permute-start | bytes 3145736 | tf_op jit(solution)/shard_map/ppermute | solution.py:190
  1407.2 46.0 %collective-permute-start.17 = (f32[512,64,8]{0,2,1:T(8,128)S(1)}, f32[512,64,8]{0,2,1:T(8,128)S(1)}, u32[]{:S(2)}, u32[]{:S(2)}) collective-permute-start(f32[512,64,8]{0,2,1:T(8,128)S(1)} %get-tuple-element.43), channel_id=1, source_target_pairs={{0,3},{1,2},{2,1},{3,0},{4,7},{5,6},{6,5},{7,4},{8,11},{9,10},{10,... | collective-permute-start | bytes 3145736 | tf_op jit(solution)/shard_map/ppermute | solution.py:190
  1407.2 46.6 %collective-permute-start.18 = (f32[512,64,8]{0,2,1:T(8,128)S(1)}, f32[512,64,8]{0,2,1:T(8,128)S(1)}, u32[]{:S(2)}, u32[]{:S(2)}) collective-permute-start(f32[512,64,8]{0,2,1:T(8,128)S(1)} %get-tuple-element.42), channel_id=1, source_target_pairs={{0,4},{1,5},{2,6},{3,7},{4,0},{5,1},{6,2},{7,3},{8,12},{9,13},{10,... | collective-permute-start | bytes 3145736 | tf_op jit(solution)/shard_map/ppermute | solution.py:190
  1409.0 90.3 %collective-permute-start.19 = (f32[512,64,8]{0,2,1:T(8,128)S(1)}, f32[512,64,8]{0,2,1:T(8,128)S(1)}, u32[]{:S(2)}, u32[]{:S(2)}) collective-permute-start(f32[512,64,8]{0,2,1:T(8,128)S(1)} %get-tuple-element.41), channel_id=1, source_target_pairs={{0,5},{1,4},{2,7},{3,6},{4,1},{5,0},{6,3},{7,2},{8,13},{9,12},{10,... | collective-permute-start | bytes 3145736 | tf_op jit(solution)/shard_map/ppermute | solution.py:190
  1410.8 89.2 %collective-permute-start.20 = (f32[512,64,8]{0,2,1:T(8,128)S(1)}, f32[512,64,8]{0,2,1:T(8,128)S(1)}, u32[]{:S(2)}, u32[]{:S(2)}) collective-permute-start(f32[512,64,8]{0,2,1:T(8,128)S(1)} %get-tuple-element.40), channel_id=1, source_target_pairs={{0,6},{1,7},{2,4},{3,5},{4,2},{5,3},{6,0},{7,1},{8,14},{9,15},{10,... | collective-permute-start | bytes 3145736 | tf_op jit(solution)/shard_map/ppermute | solution.py:190
  1431.2 69.5 %collective-permute-start.21 = (f32[512,64,8]{0,2,1:T(8,128)S(1)}, f32[512,64,8]{0,2,1:T(8,128)S(1)}, u32[]{:S(2)}, u32[]{:S(2)}) collective-permute-start(f32[512,64,8]{0,2,1:T(8,128)S(1)} %get-tuple-element.39), channel_id=1, source_target_pairs={{0,7},{1,6},{2,5},{3,4},{4,3},{5,2},{6,1},{7,0},{8,15},{9,14},{10,... | collective-permute-start | bytes 3145736 | tf_op jit(solution)/shard_map/ppermute | solution.py:190
  1520.2 34.1 %copy-start.10 = (f32[512,512]{1,0:T(8,128)S(1)}, f32[512,512]{1,0:T(8,128)}, u32[]{:S(2)}) copy-start(f32[512,512]{1,0:T(8,128)} %copy-done.9) | copy-start | bytes 3145732
  1811.4 102.4 %slice-start.6 = ((s8[8388608]{0:T(1024)(128)(4,1)}), s8[4194304]{0:T(1024)(128)(4,1)S(1)}, s32[]{:S(2)}) async-start(s8[8388608]{0:T(1024)(128)(4,1)} %bitcast.88), calls=%async_computation.12 | async-start | bytes 8388608
  1909.4 4.4 slice-start.7
  1982.5 15.8 copy-start.4
  1983.9 6.4 collective-permute-start.22
  1985.5 6.4 collective-permute-start.23
  1992.9 4.3 collective-permute-start.24
  1994.2 4.0 collective-permute-start.25
  2091.0 12.0 copy-start.8
